TPU v7x, 32 devices: a whole 2x2x4 slice. The times are simulated.
32 devices in a mesh: groups: 2 (over x), grid: 8 (over z, y), layer: 2 (over core).
Axes of the slice: x: 2, y: 2, z: 4, core: 2. Of those that a mesh axis runs over, the one named last changes fastest.
Arguments:
- density: float32 [2048, 1024], P(('groups', 'grid'), 'layer'), parts along dimension 0, as said below
- pattern: int32 [8, 8], replicated, may hold values from 0 to 1, as said below
- branch: int32 [8], replicated, may hold values from 0 to 1
- keep_blocks: int32 [8, 8], replicated, may hold values from 0 to 1, as said below
Outputs:
- purified: float32 [2048, 1024], P(('groups', 'grid'), 'layer'), parts along dimension 0
- occupation: float32 [2], P('groups'), parts along dimension 0
There are 2 independent parts, one for each index of `groups`. A program takes and returns all parts, laid end to end along the dimension named above; an argument that names none is the same for every part. Nothing has to cross between parts.
Inputs may be any that keep to these rules, and one draw needn't show every extreme that they name: density is symmetric. pattern is symmetric, holds only 0 and 1, has ones on its diagonal, and each of its rows holds exactly 3 ones. keep_blocks is symmetric, holds only 0 and 1 and has ones on its diagonal.
All inputs are finite; a program needn't handle non-finite values.
Results may differ from a plain program's by a relative error of at most 0.0003.
Values sent between devices are 32-bit elements; how exact they have to be, the bound alone decides.
A program may use at most 128 MiB of HBM per device.

v0:
```python
import jax
import jax.numpy as jnp
from jax import lax
from jax.sharding import PartitionSpec as P

BLOCK = 128


def block_mask(block_table, row_first, row_count, col_first, col_count):
    nblocks = block_table.shape[0]
    block_ids = jnp.arange(nblocks, dtype=jnp.int32)
    row_ids = (row_first + jnp.arange(row_count, dtype=jnp.int32)) // BLOCK
    col_ids = (col_first + jnp.arange(col_count, dtype=jnp.int32)) // BLOCK
    row_hot = (row_ids[:, None] == block_ids[None, :]).astype(jnp.float32)
    col_hot = (col_ids[:, None] == block_ids[None, :]).astype(jnp.float32)
    picked_rows = jnp.dot(
        row_hot,
        block_table.astype(jnp.float32),
        precision=lax.Precision.HIGHEST,
        preferred_element_type=jnp.float32,
    )
    return lax.dot_general(
        picked_rows,
        col_hot,
        (((1,), (1,)), ((), ())),
        precision=lax.Precision.HIGHEST,
        preferred_element_type=jnp.float32,
    )


def row_flags(branch, row_first, row_count):
    block_ids = jnp.arange(branch.shape[0], dtype=jnp.int32)
    row_ids = (row_first + jnp.arange(row_count, dtype=jnp.int32)) // BLOCK
    row_hot = (row_ids[:, None] == block_ids[None, :]).astype(jnp.float32)
    return jnp.dot(
        row_hot,
        branch.astype(jnp.float32),
        precision=lax.Precision.HIGHEST,
        preferred_element_type=jnp.float32,
    )


def shards(density, pattern, branch, keep_blocks):
    row_count, col_count = density.shape
    grid_index = lax.axis_index("grid")
    layer_index = lax.axis_index("layer")
    row_first = grid_index * row_count
    col_first = layer_index * col_count
    order_total = row_count * lax.axis_size("grid")
    masked = density * block_mask(pattern, row_first, row_count, col_first, col_count)
    on_diagonal = (row_first + jnp.arange(row_count, dtype=jnp.int32))[:, None] == (
        col_first + jnp.arange(col_count, dtype=jnp.int32)
    )[None, :]
    flags = row_flags(branch, row_first, row_count)
    partial_terms = lax.dot_general(
        masked,
        lax.all_gather(masked, "grid", axis=0, tiled=True),
        (((1,), (1,)), ((), ())),
        precision=lax.Precision.HIGHEST,
        preferred_element_type=jnp.float32,
    )
    product = lax.psum_scatter(partial_terms, "layer", scatter_dimension=1, tiled=True)
    chosen = jnp.where(flags[:, None] > 0.5, 2.0 * masked - product, product)
    purified = chosen * block_mask(keep_blocks, row_first, row_count, col_first, col_count)
    diag_total = lax.psum(jnp.sum(jnp.where(on_diagonal, purified, 0.0)), ("grid", "layer"))
    occupation = (diag_total / order_total).reshape(1)
    return (purified, occupation)


def solution(mesh):
    placed = (P(("groups", "grid"), "layer"), P(), P(), P())
    return jax.shard_map(
        shards,
        mesh=mesh,
        in_specs=placed,
        out_specs=(P(("groups", "grid"), "layer"), P("groups")),
        check_vma=False,
    )
```

profile of v0, /device:TPU:0, one launch (start us, length us, event | category | flops | bytes accessed | tf_op | source)
XLA Modules:
  0.0 119.8 jit_solution(8754422022923038456)
XLA Ops:
  7.2 0.0 all-gather.2.cloned.1.call-start
  7.2 0.9 fusion.4
  8.2 0.0 copy-start.2
  8.2 0.0 copy-start.1
  8.2 2.0 %convolution_multiply_fusion.1 = f32[128,512]{1,0:T(8,128)} fusion(f32[128,512]{1,0:T(8,128)} %param.4, f32[128,8]{1,0:T(8,128)S(1)} %fusion.4, s32[512]{0:T(512)S(1)} %add_select_fusion), kind=kOutput, calls=%fused_computation.1 | convolution fusion | flops 6361088 | bytes 530432 | tf_op jit(solution)/shard_map/dot_general | solution.py:22
  10.2 0.0 copy-start
  10.2 0.0 all-gather.2.cloned.1.call-update
  10.3 0.0 reduce-scatter.2.cloned.1.call-start
  10.3 52.4 %all-gather.2.cloned.1.call-done = f32[1024,512]{1,0:T(8,128)} async-done(((f32[128,512]{1,0:T(8,128)}), f32[1024,512]{1,0:T(8,128)}) %all-gather.2.cloned.1.call-update) | async-done | bytes 2097168 | tf_op jit(solution)/shard_map/all_gather | solution.py:57
  62.7 4.7 %fusion.15 = f32[128,1024]{1,0:T(8,128)} fusion(f32[128,512]{1,0:T(8,128)} %convolution_multiply_fusion.1, f32[1024,512]{1,0:T(8,128)} %all-gather.2.cloned.1.call-done), kind=kOutput, calls=%fused_computation.33 | convolution fusion | flops 805306368 | bytes 2883584 | tf_op jit(solution)/shard_map/dot_general | solution.py:55
  67.4 0.0 reduce-scatter.2.cloned.1.call-update
  67.5 0.0 copy-done.2
  67.5 0.2 fusion
  67.7 0.0 copy-done.1
  67.7 0.3 fusion.3
  68.0 6.1 %reduce-scatter.2.cloned.1.call-done = f32[128,512]{1,0:T(8,128)} async-done(((f32[128,1024]{1,0:T(8,128)}), f32[128,512]{1,0:T(8,128)}) %reduce-scatter.2.cloned.1.call-update) | async-done | bytes 262160 | tf_op jit(solution)/shard_map/reduce_scatter | solution.py:62
  74.1 0.0 copy-done
  74.1 2.6 %select_reduce_fusion = (f32[]{:T(128)}, f32[128,512]{1,0:T(8,128)}) fusion(s32[512]{0:T(512)S(1)} %iota_add_fusion, s32[128]{0:T(128)S(1)} %iota_add_fusion.1, f32[128,8]{1,0:T(8,128)S(1)} %fusion.3, s32[512]{0:T(512)S(1)} %add_select_fusion, f32[128,512]{1,0:T(8,128)} %reduce-scatter.2.cloned.1.call-done, f32[128,512]{1,0:T(8,128)S(1)} %copy-done, ...), kind=kOutput, calls=%fused_computation.5 | convolution fusion | flops 6754303 | bytes 795268 | tf_op jit(solution)/shard_map/dot_general | solution.py:22
  76.7 34.5 %psum.7 = f32[]{:T(128)} all-reduce(f32[]{:T(128)} %get-tuple-element.2), channel_id=1, replica_groups=mesh['groups'=2,'grid'=8,'layer'=2] {'grid','layer'}, use_global_device_ids=true, to_apply=%region_2.3 | all-reduce | flops 1 | bytes 8 | tf_op jit(solution)/shard_map/psum | solution.py:65
  (4 shorter events, 0.0 us)
Async XLA Ops:
  7.2 55.6 %all-gather.2.cloned.1.call-start = ((), (), s32[]{:S(2)}) async-start(), calls=%async_computation.1 | async-start | bytes 2359296 | tf_op jit(solution)/shard_map/all_gather | solution.py:57
  8.2 59.3 %copy-start.2 = (s32[8]{0:T(128)S(1)}, s32[8]{0:T(128)}, u32[]{:S(2)}) copy-start(s32[8]{0:T(128)} %param.6) | copy-start | bytes 100
  8.2 59.5 %copy-start.1 = (s32[8,8]{1,0:T(8,128)S(1)}, s32[8,8]{1,0:T(8,128)}, u32[]{:S(2)}) copy-start(s32[8,8]{1,0:T(8,128)} %param.7) | copy-start | bytes 772
  10.2 63.8 %copy-start = (f32[128,512]{1,0:T(8,128)S(1)}, f32[128,512]{1,0:T(8,128)}, u32[]{:S(2)}) copy-start(f32[128,512]{1,0:T(8,128)} %convolution_multiply_fusion.1) | copy-start | bytes 786436
  10.3 63.8 %reduce-scatter.2.cloned.1.call-start = ((), (), s32[]{:S(2)}) async-start(), calls=%async_computation.2 | async-start | bytes 786432 | tf_op jit(solution)/shard_map/reduce_scatter | solution.py:62
Sparse Core Ops, SparseCore 0:
  10.7 51.9 all-gather.1
  67.6 6.4 reduce-scatter.1
where the time goes:
time: 120 us
  waiting for transfers between devices  58.5 us (49%)
  blocking collectives  34.5 us (29%)
  between operations  15.9 us (13%)
  matrix products  10.8 us (9%)
    all_gather x1, waiting for transfers between devices, shards(): lax.all_gather(masked, 'grid', axis=0, tiled=True)  52.4 us
    psum x1, blocking collectives, shards(): lax.psum(jnp.sum(jnp.where(on_diagonal, purified, 0.0)), ('grid', 'layer'))  34.5 us
    reduce_scatter x1, waiting for transfers between devices, shards(): lax.psum_scatter(partial_terms, 'layer', scatter_dimension=1, tiled=True)  6.06 us
    dot_general x1, matrix products, shards(): lax.dot_general(masked, lax.all_gather(masked, 'grid', axis=0, tiled=True...  4.72 us
    dot_general x2, matrix products, block_mask(): lax.dot_general(picked_rows, col_hot, (((1,), (1,)), ((), ())), precision...  4.66 us
  transfers between devices with their start and end apart: 2, of which 2 were waited for; matrix products, arithmetic and copies ran while one was open for 0% of the time, Pallas kernels for 0%

commit v1 on v0

v1 whole, which is shorter than its diff:
```python
import functools

import jax
import jax.numpy as jnp
from jax import lax
from jax.experimental import pallas as pl
from jax.experimental.pallas import tpu as pltpu
from jax.sharding import PartitionSpec as P

BLOCK = 128
HALF = BLOCK // 2
PICKS = 3
MESH = pl.DeviceIdType.MESH


def kernel(
    zsize, ysize, pat, branch, keep, x, out, occ,
    full, mine, buf, sel, bhi, blo, local_sem, ex_sem, send_sem, recv_sem,
):
    n = zsize * ysize
    cols = x.shape[1]
    per = cols // BLOCK
    g = lax.axis_index("grid")
    l = lax.axis_index("layer")
    other = 1 - l
    z = g // ysize
    y = g % ysize

    own_cols = pl.ds(pl.multiple_of(l * cols, BLOCK), cols)
    own_rows = pl.ds(pl.multiple_of(l * HALF, 8), HALF)
    other_rows = pl.ds(pl.multiple_of(other * HALF, 8), HALF)
    load_half = pltpu.make_async_copy(x.at[own_rows, :], full.at[:, own_cols], local_sem.at[0])
    load_half.start()
    load_all = pltpu.make_async_copy(x, mine, local_sem.at[1])
    load_all.start()

    up_ok, down_ok = z + 1 < zsize, z > 0
    up, down = (z + 1) * ysize + y, (z - 1) * ysize + y
    across = z * ysize + (1 - y)

    barrier = pltpu.get_barrier_semaphore()
    pl.semaphore_signal(barrier, inc=1, device_id={"layer": other}, device_id_type=MESH)
    if ysize == 2:
        pl.semaphore_signal(barrier, inc=1, device_id={"grid": across}, device_id_type=MESH)

    @pl.when(up_ok)
    def _():
        pl.semaphore_signal(barrier, inc=1, device_id={"grid": up}, device_id_type=MESH)

    @pl.when(down_ok)
    def _():
        pl.semaphore_signal(barrier, inc=1, device_id={"grid": down}, device_id_type=MESH)

    peers = ysize + up_ok.astype(jnp.int32) + down_ok.astype(jnp.int32)
    pl.semaphore_wait(barrier, peers)

    exchange = pltpu.make_async_remote_copy(
        src_ref=x.at[other_rows, :], dst_ref=full.at[:, own_cols],
        send_sem=ex_sem.at[0], recv_sem=ex_sem.at[1],
        device_id={"layer": other}, device_id_type=MESH,
    )
    exchange.start()

    def picks(row):
        count = jnp.int32(0)
        found = [jnp.int32(0)] * PICKS
        for j in range(n):
            here = pat[row, j]
            for s in range(PICKS):
                found[s] = jnp.where((here == 1) & (count == s), j, found[s])
            count = count + here
        return found

    near = picks(g)
    flag = branch[g]
    zero = jnp.int32(0)
    link = []
    for s in range(PICKS):
        link.append([
            sum((jnp.where(near[s] == j, pat[j, c], zero) for j in range(n)), zero)
            for c in range(n)
        ])
    sel[...] = jnp.zeros(sel.shape, jnp.float32)

    def choose(h, gp):
        for s in range(PICKS):
            piece = buf[h, gp, :PICKS * HALF, :]
            sel[s, h] = jnp.where(near[s] == gp, piece, sel[s, h])

    def piece_copy(way, target, gp):
        return pltpu.make_async_remote_copy(
            src_ref=buf.at[l, gp], dst_ref=buf.at[l, gp],
            send_sem=send_sem.at[way, gp], recv_sem=recv_sem.at[l, gp],
            device_id=target, device_id_type=MESH,
        )

    def to_up(gp):
        return piece_copy(0, {"grid": up}, gp)

    def to_down(gp):
        return piece_copy(1, {"grid": down}, gp)

    def to_across(gp):
        return piece_copy(2, {"grid": across}, gp)

    def to_core(gp):
        return piece_copy(3, {"layer": other}, gp)

    def arrived(h, gp):
        pltpu.make_async_remote_copy(
            src_ref=buf.at[h, gp], dst_ref=buf.at[h, gp],
            send_sem=send_sem.at[3, gp], recv_sem=recv_sem.at[h, gp],
            device_id={"layer": other}, device_id_type=MESH,
        ).wait_recv()

    load_half.wait()
    exchange.wait()

    squares = jnp.zeros((8, BLOCK), jnp.float32)
    for s in range(PICKS):
        block = jnp.zeros((HALF, BLOCK), jnp.float32)
        for j in range(n):
            block = jnp.where(near[s] == j, full[:, j * BLOCK:(j + 1) * BLOCK], block)
        buf[l, g, s * HALF:(s + 1) * HALF, :] = block
        squares = squares + jnp.sum((block * block).reshape(HALF // 8, 8, BLOCK), axis=0)
    diagonal = full[:, pl.ds(pl.multiple_of(g * BLOCK, BLOCK), BLOCK)]
    at_row = lax.broadcasted_iota(jnp.int32, (HALF, BLOCK), 0) + l * HALF
    at_col = lax.broadcasted_iota(jnp.int32, (HALF, BLOCK), 1)
    diagonal = jnp.where(at_row == at_col, diagonal, 0.0)
    twice = 2.0 * jnp.sum(diagonal.reshape(HALF // 8, 8, BLOCK), axis=0)
    buf[l, g, PICKS * HALF:, :] = jnp.where(flag == 1, twice - squares, squares)

    @pl.when(up_ok)
    def _():
        to_up(g).start()

    @pl.when(down_ok)
    def _():
        to_down(g).start()

    if ysize == 2:
        to_across(g).start()
    to_core(g).start()
    choose(l, g)

    def column(d, yy, act):
        def at(zz):
            act(zz * ysize + yy)

        if d == 0:
            at(z)
            return

        @pl.when(z - d >= 0)
        def _():
            at(z - d)

        @pl.when(z + d < zsize)
        def _():
            at(z + d)

    def across_arrives(gp):
        arrived(l, gp)
        to_core(gp).start()
        choose(l, gp)

    def core_arrives(gp):
        arrived(other, gp)
        choose(other, gp)

    for d in range(1, zsize + 1):
        if d < zsize:
            @pl.when(z - d >= 0)
            def _(d=d):
                gp = (z - d) * ysize + y
                arrived(l, gp)

                @pl.when(up_ok)
                def _():
                    to_up(gp).start()

                if ysize == 2:
                    to_across(gp).start()
                to_core(gp).start()
                choose(l, gp)

            @pl.when(z + d < zsize)
            def _(d=d):
                gp = (z + d) * ysize + y
                arrived(l, gp)

                @pl.when(down_ok)
                def _():
                    to_down(gp).start()

                if ysize == 2:
                    to_across(gp).start()
                to_core(gp).start()
                choose(l, gp)

        if ysize == 2:
            column(d - 1, 1 - y, across_arrives)
        column(d - 1, y, core_arrives)
        if ysize == 2 and d > 1:
            column(d - 2, 1 - y, core_arrives)
    if ysize == 2:
        column(zsize - 1, 1 - y, core_arrives)
    load_all.wait()

    total = jnp.zeros((8, BLOCK), jnp.float32)
    for gp in range(n):
        for h in range(2):
            total = total + buf[h, gp, PICKS * HALF:, :]
    occ[0] = jnp.sum(total) * (1.0 / (n * BLOCK))

    def split(value):
        high = value.astype(jnp.bfloat16)
        return high, (value - high.astype(jnp.float32)).astype(jnp.bfloat16)

    for s in range(PICKS):
        count = zero
        counts = []
        for c in range(n):
            counts.append(count)
            count = count + link[s][c]
        for c in range(per):
            here = jnp.where(l == 0, link[s][c], link[s][per + c])
            slot = jnp.where(l == 0, counts[c], counts[per + c])
            slot = jnp.where(here == 1, slot, PICKS)
            for h in range(2):
                block = jnp.zeros((HALF, BLOCK), jnp.float32)
                for q in range(PICKS):
                    block = jnp.where(slot == q, sel[s, h, q * HALF:(q + 1) * HALF, :], block)
                high, low = split(block)
                rows = slice(s * BLOCK + h * HALF, s * BLOCK + (h + 1) * HALF)
                bhi[rows, c * BLOCK:(c + 1) * BLOCK] = high
                blo[rows, c * BLOCK:(c + 1) * BLOCK] = low

    ahi, alo = [], []
    for s in range(PICKS):
        block = jnp.concatenate(
            [buf[h, g, s * HALF:(s + 1) * HALF, :] for h in range(2)], axis=0
        )
        high, low = split(block)
        ahi.append(high)
        alo.append(low)
    ahi = jnp.concatenate(ahi, axis=1)
    alo = jnp.concatenate(alo, axis=1)
    dot = functools.partial(jnp.dot, preferred_element_type=jnp.float32)
    wide = min(cols, 512)
    for w in range(cols // wide):
        span = slice(w * wide, (w + 1) * wide)
        high, low = bhi[:, span], blo[:, span]
        product = dot(ahi, high) + (dot(ahi, low) + dot(alo, high))
        for i in range(wide // BLOCK):
            c = w * (wide // BLOCK) + i
            col = slice(c * BLOCK, (c + 1) * BLOCK)
            part = product[:, i * BLOCK:(i + 1) * BLOCK]
            masked = jnp.where(pat[g, l * per + c] == 1, mine[:, col], 0.0)
            chosen = jnp.where(flag == 1, 2.0 * masked - part, part)
            out[:, col] = jnp.where(keep[g, l * per + c] == 1, chosen, 0.0)

    if ysize == 2:
        to_across(g).wait_send()
    for gp in range(n):
        zz, yy = gp // ysize, gp % ysize
        to_core(gp).wait_send()

        @pl.when((yy == y) & (zz <= z) & up_ok)
        def _(gp=gp):
            to_up(gp).wait_send()

        @pl.when((yy == y) & (zz >= z) & down_ok)
        def _(gp=gp):
            to_down(gp).wait_send()

        if ysize == 2:
            @pl.when((yy == y) & (zz != z))
            def _(gp=gp):
                to_across(gp).wait_send()


def shards(zsize, ysize, density, pattern, branch, keep_blocks):
    rows, cols = density.shape
    n = zsize * ysize
    smem = pl.BlockSpec(memory_space=pltpu.SMEM)
    return pl.pallas_call(
        functools.partial(kernel, zsize, ysize),
        out_shape=(
            jax.ShapeDtypeStruct((rows, cols), jnp.float32),
            jax.ShapeDtypeStruct((1,), jnp.float32),
        ),
        in_specs=[smem, smem, smem, pl.BlockSpec(memory_space=pl.ANY)],
        out_specs=(pl.BlockSpec(memory_space=pltpu.VMEM), smem),
        scratch_shapes=[
            pltpu.VMEM((HALF, 2 * cols), jnp.float32),
            pltpu.VMEM((rows, cols), jnp.float32),
            pltpu.VMEM((2, n, PICKS * HALF + 8, BLOCK), jnp.float32),
            pltpu.VMEM((PICKS, 2, PICKS * HALF, BLOCK), jnp.float32),
            pltpu.VMEM((PICKS * BLOCK, cols), jnp.bfloat16),
            pltpu.VMEM((PICKS * BLOCK, cols), jnp.bfloat16),
            pltpu.SemaphoreType.DMA((2,)),
            pltpu.SemaphoreType.DMA((2,)),
            pltpu.SemaphoreType.DMA((4, n)),
            pltpu.SemaphoreType.DMA((2, n)),
        ],
        compiler_params=pltpu.CompilerParams(
            collective_id=0, has_side_effects=True, vmem_limit_bytes=40 * 1024 * 1024
        ),
        name="sp2",
    )(pattern, branch, keep_blocks, density)


def solution(mesh):
    n = mesh.shape["grid"]
    ysize = 2 if n == 8 else 1
    placed = (P(("groups", "grid"), "layer"), P(), P(), P())
    return jax.shard_map(
        functools.partial(shards, n // ysize, ysize),
        mesh=mesh,
        in_specs=placed,
        out_specs=(P(("groups", "grid"), "layer"), P("groups")),
        check_vma=False,
    )
```

time: 120 us -> 30.3 us (0.25)
  the two profiles are of different devices: /device:TPU:0 before, /device:TPU:1 now
where the time goes in v1:
time: 30.3 us; the launch traced here: 30.1 us
  Pallas kernels  24 us (79%)
  local copies, waits for them, and re-layouts  3.68 us (12%)
  between operations  2.4 us (8%)
    pallas_call x1, Pallas kernels, shards(): pl.pallas_call(functools.partial(kernel, zsize, ysize), out_shape=(jax.Sh...  24 us
    unnamed x9, local copies, waits for them, and re-layouts  3.68 us

profile of v1, /device:TPU:1, one launch (start us, length us, event | category | flops | bytes accessed | tf_op | source)
XLA Modules:
  0.0 30.1 jit_solution(3404888789823742521)
XLA Ops:
  0.6 0.0 copy-start
  0.6 0.9 %copy-done = f32[128,512]{1,0:T(8,128)S(1)} copy-done((f32[128,512]{1,0:T(8,128)S(1)}, f32[128,512]{1,0:T(8,128)}, u32[]{:S(2)}) %copy-start) | copy-done | bytes 262168
  1.6 0.0 copy-start.1
  1.6 0.7 %copy-done.1 = s32[8,8]{1,0:T(8,128)S(1)} copy-done((s32[8,8]{1,0:T(8,128)S(1)}, s32[8,8]{1,0:T(8,128)}, u32[]{:S(2)}) %copy-start.1) | copy-done | bytes 280
  2.3 0.0 copy-start.2
  2.3 0.7 %copy-done.2 = s32[8,8]{1,0:T(8,128)S(1)} copy-done((s32[8,8]{1,0:T(8,128)S(1)}, s32[8,8]{1,0:T(8,128)}, u32[]{:S(2)}) %copy-start.2) | copy-done | bytes 280
  3.0 0.0 copy-start.3
  3.0 0.7 %copy-done.3 = s32[8]{0:T(128)S(1)} copy-done((s32[8]{0:T(128)S(1)}, s32[8]{0:T(128)}, u32[]{:S(2)}) %copy-start.3) | copy-done | bytes 56
  3.6 24.0 %sp2.1 = (f32[128,512]{1,0:T(8,128)S(1)}, f32[1]{0:T(128)}) custom-call(s32[8,8]{1,0:T(8,128)S(1)} %copy-done.1, s32[8]{0:T(128)S(1)} %copy-done.3, s32[8,8]{1,0:T(8,128)S(1)} %copy-done.2, f32[128,512]{1,0:T(8,128)S(1)} %copy-done), custom_call_target="tpu_custom_call" | custom-call | tf_op jit(solution)/shard_map/sp2/pallas_call | solution.py:287
  27.6 0.7 %copy.8 = f32[128,512]{1,0:T(8,128)} copy(f32[128,512]{1,0:T(8,128)S(1)} %get-tuple-element.4) | data formatting | bytes 524288
Async XLA Ops:
  0.6 1.0 %copy-start = (f32[128,512]{1,0:T(8,128)S(1)}, f32[128,512]{1,0:T(8,128)}, u32[]{:S(2)}) copy-start(f32[128,512]{1,0:T(8,128)} %x.1) | copy-start | bytes 786436
  1.6 0.7 %copy-start.1 = (s32[8,8]{1,0:T(8,128)S(1)}, s32[8,8]{1,0:T(8,128)}, u32[]{:S(2)}) copy-start(s32[8,8]{1,0:T(8,128)} %pat.1) | copy-start | bytes 772
  2.3 0.7 %copy-start.2 = (s32[8,8]{1,0:T(8,128)S(1)}, s32[8,8]{1,0:T(8,128)}, u32[]{:S(2)}) copy-start(s32[8,8]{1,0:T(8,128)} %keep.1) | copy-start | bytes 772
  3.0 0.7 %copy-start.3 = (s32[8]{0:T(128)S(1)}, s32[8]{0:T(128)}, u32[]{:S(2)}) copy-start(s32[8]{0:T(128)} %branch.1) | copy-start | bytes 100

commit v2 on v1

--- a/solution.py
+++ b/solution.py
@@ -10,11 +10,13 @@
 BLOCK = 128
 HALF = BLOCK // 2
 PICKS = 3
+CHUNKS = (slice(0, 96), slice(96, PICKS * HALF + 8))
 MESH = pl.DeviceIdType.MESH
 
 
 def kernel(
-    zsize, ysize, pat, branch, keep, x, out, occ,
+    zsize, ysize, pat_in, branch_in, keep_in, x, out, occ,
+    pat, branch, keep,
     full, mine, buf, sel, bhi, blo, local_sem, ex_sem, send_sem, recv_sem,
 ):
     n = zsize * ysize
@@ -34,6 +36,13 @@
     load_all = pltpu.make_async_copy(x, mine, local_sem.at[1])
     load_all.start()
 
+    tables = [
+        pltpu.make_async_copy(source, held, local_sem.at[2 + i])
+        for i, (source, held) in enumerate(((pat_in, pat), (branch_in, branch), (keep_in, keep)))
+    ]
+    for table in tables:
+        table.start()
+
     up_ok, down_ok = z + 1 < zsize, z > 0
     up, down = (z + 1) * ysize + y, (z - 1) * ysize + y
     across = z * ysize + (1 - y)
@@ -71,6 +80,8 @@
             count = count + here
         return found
 
+    for table in tables:
+        table.wait()
     near = picks(g)
     flag = branch[g]
     zero = jnp.int32(0)
@@ -87,31 +98,27 @@
             piece = buf[h, gp, :PICKS * HALF, :]
             sel[s, h] = jnp.where(near[s] == gp, piece, sel[s, h])
 
-    def piece_copy(way, target, gp):
+    def piece_copy(way, target, h, gp, q):
         return pltpu.make_async_remote_copy(
-            src_ref=buf.at[l, gp], dst_ref=buf.at[l, gp],
-            send_sem=send_sem.at[way, gp], recv_sem=recv_sem.at[l, gp],
+            src_ref=buf.at[h, gp, CHUNKS[q]], dst_ref=buf.at[h, gp, CHUNKS[q]],
+            send_sem=send_sem.at[way, gp, q], recv_sem=recv_sem.at[h, gp, q],
             device_id=target, device_id_type=MESH,
         )
 
-    def to_up(gp):
-        return piece_copy(0, {"grid": up}, gp)
-
-    def to_down(gp):
-        return piece_copy(1, {"grid": down}, gp)
-
-    def to_across(gp):
-        return piece_copy(2, {"grid": across}, gp)
-
-    def to_core(gp):
-        return piece_copy(3, {"layer": other}, gp)
-
-    def arrived(h, gp):
-        pltpu.make_async_remote_copy(
-            src_ref=buf.at[h, gp], dst_ref=buf.at[h, gp],
-            send_sem=send_sem.at[3, gp], recv_sem=recv_sem.at[h, gp],
-            device_id={"layer": other}, device_id_type=MESH,
-        ).wait_recv()
+    def to_up(gp, q):
+        return piece_copy(0, {"grid": up}, l, gp, q)
+
+    def to_down(gp, q):
+        return piece_copy(1, {"grid": down}, l, gp, q)
+
+    def to_across(gp, q):
+        return piece_copy(2, {"grid": across}, l, gp, q)
+
+    def to_core(gp, q):
+        return piece_copy(3, {"layer": other}, l, gp, q)
+
+    def arrived(h, gp, q):
+        piece_copy(3, {"layer": other}, h, gp, q).wait_recv()
 
     load_half.wait()
     exchange.wait()
@@ -130,17 +137,18 @@
     twice = 2.0 * jnp.sum(diagonal.reshape(HALF // 8, 8, BLOCK), axis=0)
     buf[l, g, PICKS * HALF:, :] = jnp.where(flag == 1, twice - squares, squares)
 
-    @pl.when(up_ok)
-    def _():
-        to_up(g).start()
-
-    @pl.when(down_ok)
-    def _():
-        to_down(g).start()
-
-    if ysize == 2:
-        to_across(g).start()
-    to_core(g).start()
+    for q in range(len(CHUNKS)):
+        @pl.when(up_ok)
+        def _(q=q):
+            to_up(g, q).start()
+
+        @pl.when(down_ok)
+        def _(q=q):
+            to_down(g, q).start()
+
+        if ysize == 2:
+            to_across(g, q).start()
+        to_core(g, q).start()
     choose(l, g)
 
     def column(d, yy, act):
@@ -160,43 +168,39 @@
             at(z + d)
 
     def across_arrives(gp):
-        arrived(l, gp)
-        to_core(gp).start()
+        for q in range(len(CHUNKS)):
+            arrived(l, gp, q)
+            to_core(gp, q).start()
         choose(l, gp)
 
     def core_arrives(gp):
-        arrived(other, gp)
+        for q in range(len(CHUNKS)):
+            arrived(other, gp, q)
         choose(other, gp)
+
+    def pass_on(gp, q, further, way):
+        arrived(l, gp, q)
+
+        @pl.when(further)
+        def _():
+            way(gp, q).start()
+
+        if ysize == 2:
+            to_across(gp, q).start()
+        to_core(gp, q).start()
 
     for d in range(1, zsize + 1):
         if d < zsize:
-            @pl.when(z - d >= 0)
-            def _(d=d):
-                gp = (z - d) * ysize + y
-                arrived(l, gp)
-
-                @pl.when(up_ok)
-                def _():
-                    to_up(gp).start()
-
-                if ysize == 2:
-                    to_across(gp).start()
-                to_core(gp).start()
-                choose(l, gp)
-
-            @pl.when(z + d < zsize)
-            def _(d=d):
-                gp = (z + d) * ysize + y
-                arrived(l, gp)
-
-                @pl.when(down_ok)
-                def _():
-                    to_down(gp).start()
-
-                if ysize == 2:
-                    to_across(gp).start()
-                to_core(gp).start()
-                choose(l, gp)
+            for q in range(len(CHUNKS)):
+                @pl.when(z - d >= 0)
+                def _(d=d, q=q):
+                    pass_on((z - d) * ysize + y, q, up_ok, to_up)
+
+                @pl.when(z + d < zsize)
+                def _(d=d, q=q):
+                    pass_on((z + d) * ysize + y, q, down_ok, to_down)
+
+            column(d, y, functools.partial(choose, l))
 
         if ysize == 2:
             column(d - 1, 1 - y, across_arrives)
@@ -260,24 +264,23 @@
             chosen = jnp.where(flag == 1, 2.0 * masked - part, part)
             out[:, col] = jnp.where(keep[g, l * per + c] == 1, chosen, 0.0)
 
-    if ysize == 2:
-        to_across(g).wait_send()
     for gp in range(n):
         zz, yy = gp // ysize, gp % ysize
-        to_core(gp).wait_send()
-
-        @pl.when((yy == y) & (zz <= z) & up_ok)
-        def _(gp=gp):
-            to_up(gp).wait_send()
-
-        @pl.when((yy == y) & (zz >= z) & down_ok)
-        def _(gp=gp):
-            to_down(gp).wait_send()
-
-        if ysize == 2:
-            @pl.when((yy == y) & (zz != z))
-            def _(gp=gp):
-                to_across(gp).wait_send()
+        for q in range(len(CHUNKS)):
+            to_core(gp, q).wait_send()
+
+            @pl.when((yy == y) & (zz <= z) & up_ok)
+            def _(gp=gp, q=q):
+                to_up(gp, q).wait_send()
+
+            @pl.when((yy == y) & (zz >= z) & down_ok)
+            def _(gp=gp, q=q):
+                to_down(gp, q).wait_send()
+
+            if ysize == 2:
+                @pl.when(yy == y)
+                def _(gp=gp, q=q):
+                    to_across(gp, q).wait_send()
 
 
 def shards(zsize, ysize, density, pattern, branch, keep_blocks):
@@ -290,22 +293,25 @@
             jax.ShapeDtypeStruct((rows, cols), jnp.float32),
             jax.ShapeDtypeStruct((1,), jnp.float32),
         ),
-        in_specs=[smem, smem, smem, pl.BlockSpec(memory_space=pl.ANY)],
+        in_specs=[pl.BlockSpec(memory_space=pltpu.HBM)] * 4,
         out_specs=(pl.BlockSpec(memory_space=pltpu.VMEM), smem),
         scratch_shapes=[
+            pltpu.SMEM(pattern.shape, jnp.int32),
+            pltpu.SMEM(branch.shape, jnp.int32),
+            pltpu.SMEM(keep_blocks.shape, jnp.int32),
             pltpu.VMEM((HALF, 2 * cols), jnp.float32),
             pltpu.VMEM((rows, cols), jnp.float32),
             pltpu.VMEM((2, n, PICKS * HALF + 8, BLOCK), jnp.float32),
             pltpu.VMEM((PICKS, 2, PICKS * HALF, BLOCK), jnp.float32),
             pltpu.VMEM((PICKS * BLOCK, cols), jnp.bfloat16),
             pltpu.VMEM((PICKS * BLOCK, cols), jnp.bfloat16),
+            pltpu.SemaphoreType.DMA((5,)),
             pltpu.SemaphoreType.DMA((2,)),
-            pltpu.SemaphoreType.DMA((2,)),
-            pltpu.SemaphoreType.DMA((4, n)),
-            pltpu.SemaphoreType.DMA((2, n)),
+            pltpu.SemaphoreType.DMA((4, n, len(CHUNKS))),
+            pltpu.SemaphoreType.DMA((2, n, len(CHUNKS))),
         ],
         compiler_params=pltpu.CompilerParams(
-            collective_id=0, has_side_effects=True, vmem_limit_bytes=40 * 1024 * 1024
+            collective_id=0, has_side_effects=True, vmem_limit_bytes=60 * 1024 * 1024
         ),
         name="sp2",
     )(pattern, branch, keep_blocks, density)

time: 30.3 us -> 26.8 us (0.88)
  local copies, waits for them, and re-layouts: 3.68 us -> 1.67 us
  Pallas kernels: 24 us -> 22.5 us
    unnamed x9 -> x1, local copies, waits for them, and re-layouts: 3.68 us -> 1.67 us
    pallas_call x1, Pallas kernels: 24 us -> 22.5 us  [shards(): pl.pallas_call(functools.partial(kernel, zsize, ysize), out_shape=(jax.Sh...]
where the time goes in v2:
time: 26.8 us; the launch traced here: 26.6 us
  Pallas kernels  22.5 us (84%)
  between operations  2.4 us (9%)
  local copies, waits for them, and re-layouts  1.67 us (6%)
    pallas_call x1, Pallas kernels, shards(): pl.pallas_call(functools.partial(kernel, zsize, ysize), out_shape=(jax.Sh...  22.5 us
    unnamed x1, local copies, waits for them, and re-layouts  1.67 us

profile of v2, /device:TPU:1, one launch (start us, length us, event | category | flops | bytes accessed | tf_op | source)
XLA Modules:
  0.0 26.6 jit_solution(17287879943635011365)
XLA Ops:
  0.6 22.5 %sp2.1 = (f32[128,512]{1,0:T(8,128)}, f32[1]{0:T(128)}) custom-call(s32[8,8]{1,0:T(8,128)} %pat_in.1, s32[8]{0:T(128)} %branch_in.1, s32[8,8]{1,0:T(8,128)} %keep_in.1, f32[128,512]{1,0:T(8,128)} %x.1), custom_call_target="tpu_custom_call" | custom-call | tf_op jit(solution)/shard_map/sp2/pallas_call | solution.py:290
  23.2 1.7 %copy.8 = f32[128,512]{1,0:T(8,128)} copy(f32[128,512]{1,0:T(8,128)} %get-tuple-element.4) | data formatting | bytes 524288

commit v3 on v2

--- a/solution.py
+++ b/solution.py
@@ -84,15 +84,6 @@
         table.wait()
     near = picks(g)
     flag = branch[g]
-    zero = jnp.int32(0)
-    link = []
-    for s in range(PICKS):
-        link.append([
-            sum((jnp.where(near[s] == j, pat[j, c], zero) for j in range(n)), zero)
-            for c in range(n)
-        ])
-    sel[...] = jnp.zeros(sel.shape, jnp.float32)
-
     def choose(h, gp):
         for s in range(PICKS):
             piece = buf[h, gp, :PICKS * HALF, :]
@@ -149,6 +140,15 @@
         if ysize == 2:
             to_across(g, q).start()
         to_core(g, q).start()
+    zero = jnp.int32(0)
+    link = []
+    for s in range(PICKS):
+        link.append([
+            sum((jnp.where(near[s] == j, pat[j, c], zero) for j in range(n)), zero)
+            for c in range(n)
+        ])
+    sel[...] = jnp.zeros(sel.shape, jnp.float32)
+
     choose(l, g)
 
     def column(d, yy, act):
@@ -290,7 +290,7 @@
     return pl.pallas_call(
         functools.partial(kernel, zsize, ysize),
         out_shape=(
-            jax.ShapeDtypeStruct((rows, cols), jnp.float32),
+            pltpu.VMEM((rows, cols), jnp.float32),
             jax.ShapeDtypeStruct((1,), jnp.float32),
         ),
         in_specs=[pl.BlockSpec(memory_space=pltpu.HBM)] * 4,
@@ -311,10 +311,10 @@
             pltpu.SemaphoreType.DMA((2, n, len(CHUNKS))),
         ],
         compiler_params=pltpu.CompilerParams(
-            collective_id=0, has_side_effects=True, vmem_limit_bytes=60 * 1024 * 1024
+            collective_id=0, has_side_effects=True, vmem_limit_bytes=40 * 1024 * 1024
         ),
         name="sp2",
-    )(pattern, branch, keep_blocks, density)
+    )(*(pltpu.with_memory_space_constraint(v, pltpu.HBM) for v in (pattern, branch, keep_blocks, density)))
 
 
 def solution(mesh):

time: 26.8 us -> 25.5 us (0.951)
  local copies, waits for them, and re-layouts: 1.67 us -> 0.71 us
    unnamed x1, local copies, waits for them, and re-layouts: 1.67 us -> 0.71 us
where the time goes in v3:
time: 25.5 us; the launch traced here: 25.4 us
  Pallas kernels  22.4 us (88%)
  between operations  2.33 us (9%)
  local copies, waits for them, and re-layouts  0.71 us (3%)
    pallas_call x1, Pallas kernels, shards(): pl.pallas_call(functools.partial(kernel, zsize, ysize), out_shape=(pltpu....  22.4 us
    unnamed x1, local copies, waits for them, and re-layouts  0.71 us

profile of v3, /device:TPU:1, one launch (start us, length us, event | category | flops | bytes accessed | tf_op | source)
XLA Modules:
  0.0 25.4 jit_solution(680272677636330138)
XLA Ops:
  0.6 22.4 %sp2.1 = (f32[128,512]{1,0:T(8,128)S(1)}, f32[1]{0:T(128)}) custom-call(s32[8,8]{1,0:T(8,128)} %pat_in.1, s32[8]{0:T(128)} %branch_in.1, s32[8,8]{1,0:T(8,128)} %keep_in.1, f32[128,512]{1,0:T(8,128)} %x.1), custom_call_target="tpu_custom_call" | custom-call | tf_op jit(solution)/shard_map/sp2/pallas_call | solution.py:290
  23.0 0.7 %copy.8 = f32[128,512]{1,0:T(8,128)} copy(f32[128,512]{1,0:T(8,128)S(1)} %get-tuple-element.2) | data formatting | bytes 524288

commit v4 on v3

--- a/solution.py
+++ b/solution.py
@@ -10,7 +10,7 @@
 BLOCK = 128
 HALF = BLOCK // 2
 PICKS = 3
-CHUNKS = (slice(0, 96), slice(96, PICKS * HALF + 8))
+CHUNKS = (slice(0, HALF), slice(HALF, 2 * HALF), slice(2 * HALF, PICKS * HALF + 8))
 MESH = pl.DeviceIdType.MESH
 
 

time: 25.5 us -> 25.6 us (level)
  no operation moved by 1% of the time
where the time goes in v4:
time: 25.6 us; the launch traced here: 25.4 us
  Pallas kernels  22.4 us (88%)
  between operations  2.33 us (9%)
  local copies, waits for them, and re-layouts  0.71 us (3%)
    pallas_call x1, Pallas kernels, shards(): pl.pallas_call(functools.partial(kernel, zsize, ysize), out_shape=(pltpu....  22.4 us
    unnamed x1, local copies, waits for them, and re-layouts  0.71 us

profile of v4, /device:TPU:1, one launch (start us, length us, event | category | flops | bytes accessed | tf_op | source)
XLA Modules:
  0.0 25.4 jit_solution(7024908360923382424)
XLA Ops:
  0.6 22.4 %sp2.1 = (f32[128,512]{1,0:T(8,128)S(1)}, f32[1]{0:T(128)}) custom-call(s32[8,8]{1,0:T(8,128)} %pat_in.1, s32[8]{0:T(128)} %branch_in.1, s32[8,8]{1,0:T(8,128)} %keep_in.1, f32[128,512]{1,0:T(8,128)} %x.1), custom_call_target="tpu_custom_call" | custom-call | tf_op jit(solution)/shard_map/sp2/pallas_call | solution.py:290
  23.0 0.7 %copy.8 = f32[128,512]{1,0:T(8,128)} copy(f32[128,512]{1,0:T(8,128)S(1)} %get-tuple-element.2) | data formatting | bytes 524288

commit v5 on v3

--- a/solution.py
+++ b/solution.py
@@ -200,10 +200,11 @@
                 def _(d=d, q=q):
                     pass_on((z + d) * ysize + y, q, down_ok, to_down)
 
-            column(d, y, functools.partial(choose, l))
 
         if ysize == 2:
             column(d - 1, 1 - y, across_arrives)
+        if d < zsize:
+            column(d, y, functools.partial(choose, l))
         column(d - 1, y, core_arrives)
         if ysize == 2 and d > 1:
             column(d - 2, 1 - y, core_arrives)

time: 25.5 us -> 25.5 us (level)
  no operation moved by 1% of the time
where the time goes in v5:
time: 25.5 us; the launch traced here: 25.4 us
  Pallas kernels  22.4 us (88%)
  between operations  2.33 us (9%)
  local copies, waits for them, and re-layouts  0.71 us (3%)
    pallas_call x1, Pallas kernels, shards(): pl.pallas_call(functools.partial(kernel, zsize, ysize), out_shape=(pltpu....  22.4 us
    unnamed x1, local copies, waits for them, and re-layouts  0.71 us

profile of v5, /device:TPU:1, one launch (start us, length us, event | category | flops | bytes accessed | tf_op | source)
XLA Modules:
  0.0 25.4 jit_solution(16769138728081105007)
XLA Ops:
  0.6 22.4 %sp2.1 = (f32[128,512]{1,0:T(8,128)S(1)}, f32[1]{0:T(128)}) custom-call(s32[8,8]{1,0:T(8,128)} %pat_in.1, s32[8]{0:T(128)} %branch_in.1, s32[8,8]{1,0:T(8,128)} %keep_in.1, f32[128,512]{1,0:T(8,128)} %x.1), custom_call_target="tpu_custom_call" | custom-call | tf_op jit(solution)/shard_map/sp2/pallas_call | solution.py:291
  23.0 0.7 %copy.8 = f32[128,512]{1,0:T(8,128)} copy(f32[128,512]{1,0:T(8,128)S(1)} %get-tuple-element.2) | data formatting | bytes 524288
